TPU v7x, 32 devices: a whole 2x2x4 slice. The times are simulated.
32 devices in a mesh: group: 2 (over y), walker: 4 (over z), param: 4 (over x, core).
Axes of the slice: x: 2, y: 2, z: 4, core: 2. Of those that a mesh axis runs over, the one named last changes fastest.
Arguments:
- activations: bfloat16 [96, 1024, 256], P(('group', 'walker'), 'param'), parts along dimension 0, may hold values from -6 to 6
- cotangents: bfloat16 [96, 1024, 1024], P(('group', 'walker'), 'param'), parts along dimension 0, may hold values from -0.0010036526 to 0.0010036526
- local_energy: float32 [96], P(('group', 'walker')), parts along dimension 0, may hold values from -6 to 6
- walker_ids: int32 [96], P(('group', 'walker')), parts along dimension 0, may hold values from 0 to 47, each once
- prev_direction: float32 [512, 1024], P('group', 'param'), parts along dimension 0, may hold values from -6 to 6
- column_order: int32 [2048], P('group'), parts along dimension 0, may hold values from 0 to 1023, each once
- weights: float32 [512, 1024], P('group', 'param'), parts along dimension 0, may hold values from -0.375 to 0.375
Outputs:
- direction: float32 [512, 1024], P('group', 'param'), parts along dimension 0
- new_weights: float32 [512, 1024], P('group', 'param'), parts along dimension 0
- coefficients: float32 [96], P(('group', 'walker')), parts along dimension 0
There are 2 independent parts, one for each index of `group`. A program takes and returns all parts, laid end to end along the dimension named above; each array names one. Nothing has to cross between parts.
Inputs may be any that keep to these rules, and one draw needn't show every extreme that they name: `walker_ids`: each walker id appears once. `column_order`: each column appears once.
All inputs are finite; a program needn't handle non-finite values.
Results may differ from a plain program's by a relative error of at most 0.0015.
Values may be sent and summed in bfloat16 or wider, within the bound.
A program may use at most 128 MiB of HBM per device.

v0:
```python
import jax
import jax.numpy as jnp
from jax import lax
from jax.sharding import PartitionSpec as P


def solve_system(system, zeta):
    factor = jnp.linalg.cholesky(system)
    column = zeta[:, None]
    middle = lax.linalg.triangular_solve(
        factor, column, left_side=True, lower=True, transpose_a=False
    )
    result = lax.linalg.triangular_solve(
        factor, middle, left_side=True, lower=True, transpose_a=True
    )
    return result[:, 0]


def shards(
    activations, cotangents, local_energy, walker_ids, prev_direction, column_order, weights
):
    rows = cotangents.shape[0]
    orb_local = cotangents.shape[1]
    width_in = activations.shape[2]
    walkers = rows * lax.axis_size("walker")
    walker_pos = lax.axis_index("walker")
    param_pos = lax.axis_index("param")
    grads = jnp.einsum(
        "wnd,won->wdo",
        lax.all_gather(activations, "param", axis=1, tiled=True),
        cotangents,
        preferred_element_type=jnp.float32,
    )
    flat = grads.reshape(rows, width_in * orb_local)
    column_total = lax.psum(jnp.sum(flat, axis=0), "walker")
    centered = (flat - column_total / walkers).astype(jnp.bfloat16)
    energies_all = lax.all_gather(local_energy, "walker", axis=0, tiled=True)
    energy_mean = jnp.mean(energies_all)
    centered_energy = energies_all[walker_ids] - energy_mean
    stored = lax.all_gather(prev_direction, "param", axis=1, tiled=True)
    my_order = lax.dynamic_slice_in_dim(column_order, param_pos * orb_local, orb_local)
    aligned = jnp.take(stored, my_order, axis=1)
    wide = centered.astype(jnp.float32)
    proj_part = jnp.dot(wide, aligned.reshape(-1), precision=lax.Precision.HIGHEST)
    block = lax.dot_general(
        centered,
        lax.all_gather(centered, "walker", axis=0, tiled=True),
        (((1,), (1,)), ((), ())),
        preferred_element_type=jnp.float32,
    )
    gram_mine, proj_mine = lax.psum((block, proj_part), "param")
    zeta_mine = centered_energy - 0.9 * proj_mine
    gram, zeta = (
        lax.all_gather(gram_mine, "walker", axis=0, tiled=True),
        lax.all_gather(zeta_mine, "walker", axis=0, tiled=True),
    )
    system = gram + 0.002 * jnp.eye(walkers, dtype=jnp.float32) + 1.0 / walkers
    solved = solve_system(system, zeta)
    mine = lax.dynamic_slice_in_dim(solved, walker_pos * rows, rows)
    update_part = jnp.dot(mine, wide, precision=lax.Precision.HIGHEST)
    update_total = lax.psum(update_part, "walker")
    direction = update_total.reshape(width_in, orb_local) + 0.9 * aligned
    return (direction, weights - 0.05 * direction, mine)


def solution(mesh):
    in_specs = (
        P(("group", "walker"), "param", None),
        P(("group", "walker"), "param", None),
        P(("group", "walker")),
        P(("group", "walker")),
        P("group", "param"),
        P("group"),
        P("group", "param"),
    )
    out_specs = (P("group", "param"), P("group", "param"), P(("group", "walker")))
    return jax.shard_map(shards, mesh=mesh, in_specs=in_specs, out_specs=out_specs, check_vma=False)
```

profile of v0, /device:TPU:0, one launch (start us, length us, event | category | flops | bytes accessed | tf_op | source)
XLA Modules:
  0.0 368.5 jit_solution(4993338365333594377)
XLA Ops:
  7.2 0.0 all-gather.6.cloned.1.call-start
  7.2 2.6 copy.23
  9.8 0.0 all-gather.6.cloned.1.call-update
  9.8 0.0 copy-start.1
  9.8 0.0 all-reduce.6.cloned.1.call-start
  9.9 50.0 %all-gather.6.cloned.1.call-done = bf16[12,1024,256]{1,2,0:T(8,128)(2,1)} async-done(((bf16[12,256,256]{1,2,0:T(8,128)(2,1)}), bf16[12,1024,256]{1,2,0:T(8,128)(2,1)}) %all-gather.6.cloned.1.call-update) | async-done | bytes 6291472 | tf_op jit(solution)/shard_map/all_gather | solution.py:30
  59.9 6.5 %fusion.16 = (f32[256,256]{1,0:T(8,128)S(1)}, f32[12,256,256]{2,1,0:T(8,128)S(1)}) fusion(bf16[12,1024,256]{1,2,0:T(8,128)(2,1)} %all-gather.6.cloned.1.call-done, bf16[12,256,1024]{2,1,0:T(8,128)(2,1)} %param.8), kind=kOutput, calls=%fused_computation.36 | convolution fusion | flops 1611333632 | bytes 15990784 | tf_op jit(solution)/shard_map/wnd,won->wdo/dot_general | solution.py:28
  66.3 0.8 copy.33
  67.2 0.0 all-reduce.6.cloned.1.call-update
  67.2 0.0 all-gather.8.cloned.1.call-start
  67.3 0.0 copy-done.1
  67.3 0.8 copy.25
  68.1 0.0 all-gather.8.cloned.1.call-update
  68.1 0.0 all-gather.10.cloned.1.call-start
  68.2 0.5 pad.2
  68.6 4.4 %copy.32 = f32[2,8,256,256]{3,1,2,0:T(8,128)} copy(f32[2,8,256,256]{3,2,1,0:T(8,128)S(1)} %bitcast.53) | data formatting | bytes 8388608
  73.0 29.6 %all-reduce.6.cloned.1.call-done = f32[65536]{0:T(1024)} async-done(((f32[65536]{0:T(1024)}), f32[65536]{0:T(1024)}) %all-reduce.6.cloned.1.call-update) | async-done | bytes 262160 | tf_op jit(solution)/shard_map/psum | solution.py:35
  102.7 1.0 broadcast_multiply_fusion
  103.7 0.0 copy-start.7
  103.7 0.0 copy-start.5
  103.7 0.0 copy-start.6
  103.7 3.9 %fusion.6 = bf16[1,12,65536]{2,1,0:T(8,128)(2,1)} fusion(f32[12,65536]{1,0:T(8,128)} %bitcast.51, f32[65536]{0:T(1024)S(1)} %broadcast_multiply_fusion), kind=kLoop, calls=%fused_computation.10 | loop fusion | flops 1572864 | bytes 4980736
  107.6 0.0 all-gather.10.cloned.1.call-update
  107.6 0.0 all-reduce.8.cloned.1.call-start
  107.7 0.6 dynamic-slice.1
  108.9 0.2 dynamic-update-slice.3
  109.2 10.7 %all-reduce = f32[48]{0:T(128)S(1)} all-reduce(f32[48]{0:T(128)S(1)} %dynamic-update-slice.3), channel_id=1, replica_groups=mesh['group'=2,'walker'=4,'param'=4] {'walker'}, use_global_device_ids=true, to_apply=%add | all-reduce | flops 48 | bytes 384
  119.9 0.0 copy-done.6
  119.9 0.7 gather_fusion
  120.6 0.6 reduce_sum.22
  121.8 0.8 compare_and_fusion
  122.6 0.0 all-gather.8.cloned.1.call-done
  122.7 2.9 gather_fusion.1
  125.5 1.8 select_bitcast_fusion
  127.3 1.8 copy.31
  129.1 0.8 sub.32
  129.9 1.3 subtract_convert_fusion.1
  131.2 0.2 pad.3
  131.4 1.2 copy.34
  132.6 3.1 fusion.2
  135.7 136.8 %all-gather.10.cloned.1.call-done = bf16[4,12,65536]{2,1,0:T(8,128)(2,1)} async-done(((bf16[1,12,65536]{2,1,0:T(8,128)(2,1)}), bf16[4,12,65536]{2,1,0:T(8,128)(2,1)}) %all-gather.10.cloned.1.call-update) | async-done | bytes 6291472 | tf_op jit(solution)/shard_map/all_gather | solution.py:47
  272.6 6.0 %reshape.79 = bf16[48,65536]{1,0:T(8,128)(2,1)} reshape(bf16[4,12,65536]{2,1,0:T(8,128)(2,1)} %all-gather.10.cloned.1.call-done) | data formatting | bytes 12582912
  278.6 5.8 %fusion.5 = f32[12,48]{1,0:T(8,128)S(1)} fusion(bf16[48,65536]{1,0:T(8,128)(2,1)} %reshape.79, f32[12,65536]{1,0:T(8,128)} %bitcast.52, f32[65536]{0:T(1024)S(1)} %broadcast_multiply_fusion), kind=kOutput, calls=%fused_computation.9 | convolution fusion | flops 77070336 | bytes 9701632 | tf_op jit(solution)/shard_map/dot_general | solution.py:45
  284.4 7.2 %all-reduce.2 = (f32[12,48]{1,0:T(8,128)S(1)}, f32[12]{0:T(128)S(1)}) all-reduce(f32[12,48]{1,0:T(8,128)S(1)} %fusion.5, f32[12]{0:T(128)S(1)} %fusion.2), channel_id=1, replica_groups=mesh['group'=2,'walker'=4,'param'=4] {'param'}, use_global_device_ids=true, to_apply=%region_2.0 | all-reduce | flops 588 | bytes 4704 | tf_op jit(solution)/shard_map/psum | solution.py:51
  291.6 13.1 %all-gather.1 = f32[4,12,48]{2,1,0:T(8,128)S(1)} all-gather(f32[1,12,48]{2,1,0:T(8,128)S(1)} %bitcast.59), channel_id=1, replica_groups=mesh['group'=2,'walker'=4,'param'=4] {'walker'}, dimensions={0}, use_global_device_ids=true | all-gather | bytes 11520 | tf_op jit(solution)/shard_map/all_gather | solution.py:54
  304.7 0.1 copy.24
  304.8 4.4 %cholesky.16 = f32[48,48]{1,0:T(8,128)S(1)} custom-call(f32[48,48]{1,0:T(8,128)S(1)} %fusion.11), custom_call_target="Cholesky" | custom-call | tf_op jit(solution)/shard_map/jit(cholesky)/cholesky | solution.py:8
  309.3 0.6 compare_reduce_fusion
  309.9 0.7 fusion.8
  310.6 3.7 custom-call.8
  314.2 0.1 subtract_dynamic-update-slice_fusion
  314.3 8.9 %all-reduce.1 = f32[48]{0:T(128)S(1)} all-reduce(f32[48]{0:T(128)S(1)} %subtract_dynamic-update-slice_fusion), channel_id=1, replica_groups=mesh['group'=2,'walker'=4,'param'=4] {'walker'}, use_global_device_ids=true, to_apply=%add.1 | all-reduce | flops 48 | bytes 384
  323.2 0.1 convolution_bitcast_fusion.1
  323.4 0.1 convolution_bitcast_fusion
  323.5 0.1 dynamic_slice.7
  323.6 1.0 fusion.12
  324.6 0.1 reshape.53
  324.7 0.8 copy.26
  325.5 0.0 all-reduce.8.cloned.1.call-update
  325.5 0.1 copy.27
  325.7 33.5 %all-reduce.8.cloned.1.call-done = f32[256,256]{0,1:T(8,128)} async-done(((f32[256,256]{0,1:T(8,128)}), f32[256,256]{0,1:T(8,128)}) %all-reduce.8.cloned.1.call-update) | async-done | bytes 262160 | tf_op jit(solution)/shard_map/psum | solution.py:61
  359.2 1.1 multiply_subtract_fusion
  360.3 0.8 copy.28
  361.1 0.8 copy.29
  (19 shorter events, 0.1 us)
Async XLA Ops:
  7.2 52.7 %all-gather.6.cloned.1.call-start = ((), (), s32[]{:S(2)}) async-start(), calls=%async_computation | async-start | bytes 7864320 | tf_op jit(solution)/shard_map/all_gather | solution.py:30
  9.8 57.4 %copy-start.1 = (f32[256,256]{1,0:T(8,128)S(1)}, f32[256,256]{1,0:T(8,128)}, u32[]{:S(2)}) copy-start(f32[256,256]{1,0:T(8,128)} %param.11) | copy-start | bytes 786436
  9.8 92.9 %all-reduce.6.cloned.1.call-start = ((), (), s32[]{:S(2)}) async-start(), calls=%async_computation.1 | async-start | bytes 524288 | tf_op jit(solution)/shard_map/psum | solution.py:35
  67.2 55.4 %all-gather.8.cloned.1.call-start = ((), (), s32[]{:S(2)}) async-start(), calls=%async_computation.2 | async-start | bytes 1310720 | tf_op jit(solution)/shard_map/all_gather | solution.py:40
  68.1 204.4 %all-gather.10.cloned.1.call-start = ((), (), s32[]{:S(2)}) async-start(), calls=%async_computation.4 | async-start | bytes 10485760 | tf_op jit(solution)/shard_map/all_gather | solution.py:47
  103.7 4.0 %copy-start.7 = (u32[32]{0:T(128)S(1)}, u32[32]{0:T(128)}, u32[]{:S(2)}) copy-start(u32[32]{0:T(128)} %constant.99) | copy-start | bytes 388
  103.7 5.2 %copy-start.5 = (f32[12]{0:T(128)S(1)}, f32[12]{0:T(128)}, u32[]{:S(2)}) copy-start(f32[12]{0:T(128)} %param.9) | copy-start | bytes 148
  103.7 16.2 %copy-start.6 = (s32[12]{0:T(128)S(1)}, s32[12]{0:T(128)}, u32[]{:S(2)}) copy-start(s32[12]{0:T(128)} %param.10) | copy-start | bytes 148
  107.6 251.6 %all-reduce.8.cloned.1.call-start = ((), (), s32[]{:S(2)}) async-start(), calls=%async_computation.3 | async-start | bytes 524288 | tf_op jit(solution)/shard_map/psum | solution.py:61
  131.2 1.4 copy-start.3
  284.4 41.2 %copy-start.2 = (f32[256,256]{1,0:T(8,128)S(1)}, f32[256,256]{1,0:T(8,128)}, u32[]{:S(2)}) copy-start(f32[256,256]{1,0:T(8,128)} %param.13) | copy-start | bytes 786436
  284.4 74.8 %copy-start = (f32[256,256]{1,0:T(8,128)S(1)}, f32[256,256]{1,0:T(8,128)}, u32[]{:S(2)}) copy-start(f32[256,256]{1,0:T(8,128)} %gather_fusion.1) | copy-start | bytes 786436
  323.6 38.3 %copy-start.4 = (f32[12]{0:T(128)}, f32[12]{0:T(128)S(1)}, u32[]{:S(2)}) copy-start(f32[12]{0:T(128)S(1)} %dynamic_slice.7) | copy-start | bytes 148
Sparse Core Ops, SparseCore 0:
  9.9 49.8 all-gather.5
  67.3 35.3 all-reduce.5
  104.9 16.4 all-gather.7
  122.9 149.6 all-gather.9
  325.7 33.4 all-reduce.7
where the time goes:
time: 369 us; the launch traced here: 368 us
  waiting for transfers between devices  250 us (68%)
  blocking collectives  40 us (11%)
  local copies, waits for them, and re-layouts  26.4 us (7%)
  other arithmetic  19.9 us (5%)
  matrix products  16.6 us (4%)
  between operations  15.3 us (4%)
    all_gather x1, waiting for transfers between devices, shards(): lax.all_gather(centered, 'walker', axis=0, tiled=True)  137 us
    all_gather x1, waiting for transfers between devices, shards(): lax.all_gather(activations, 'param', axis=1, tiled=True)  50 us
    psum x1, waiting for transfers between devices, shards(): update_total = lax.psum(update_part, 'walker')  33.5 us
    psum x1, waiting for transfers between devices, shards(): column_total = lax.psum(jnp.sum(flat, axis=0), 'walker')  29.6 us
    unnamed x2, blocking collectives  19.6 us
    unnamed x32, local copies, waits for them, and re-layouts  19.2 us
    all_gather x1, blocking collectives, shards(): lax.all_gather(gram_mine, 'walker', axis=0, tiled=True)  13.1 us
  transfers between devices with their start and end apart: 5, of which 4 were waited for; matrix products, arithmetic and copies ran while one was open for 7% of the time, Pallas kernels for 0%

commit v1 on v0

--- a/solution.py
+++ b/solution.py
@@ -1,7 +1,15 @@
+import functools
+
 import jax
 import jax.numpy as jnp
 from jax import lax
+from jax.experimental import pallas as pl
+from jax.experimental.pallas import tpu as pltpu
 from jax.sharding import PartitionSpec as P
+
+F32 = jnp.float32
+BF16 = jnp.bfloat16
+MESH = pl.DeviceIdType.MESH
 
 
 def solve_system(system, zeta):
@@ -16,7 +24,7 @@
     return result[:, 0]
 
 
-def shards(
+def plain_shards(
     activations, cotangents, local_energy, walker_ids, prev_direction, column_order, weights
 ):
     rows = cotangents.shape[0]
@@ -63,6 +71,436 @@
     return (direction, weights - 0.05 * direction, mine)
 
 
+def kernel(
+    act, cot, prev, order, weights, packed,
+    dir_out, w_out, coef_out,
+    agath, cbuf, sbuf, rbuf, run, runs, total, cent, stored, alig, mean_ref,
+    gred, zred, gsum, dscr, ebuf, esort, csol,
+    loc_sem, xs, xr, bs, br, fs, fr, zs, zr, ps, pr, gs, gr, hs, hr, ds, dr, es, er,
+    *, Z, PP,
+):
+    R, n, D = act.shape
+    O = cot.shape[1]
+    W = R * Z
+    X = PP // 2
+    dc = D // Z
+    L = gsum.shape[1]
+    halves = O // 128
+    z = lax.axis_index("walker")
+    p = lax.axis_index("param")
+    x = p // 2
+    c = p % 2
+    sib = x * 2 + (1 - c)
+
+    def xpeer(j):
+        return lax.rem(x + j, X) * 2 + c
+
+    def remote(src, dst, ssem, rsem, axis, idx):
+        return pltpu.make_async_remote_copy(
+            src_ref=src, dst_ref=dst, send_sem=ssem, recv_sem=rsem,
+            device_id={axis: idx}, device_id_type=MESH,
+        )
+
+    def cot_copy(r):
+        return pltpu.make_async_copy(cot.at[r], cbuf.at[r], loc_sem.at[0, r])
+
+    def act_copy(r):
+        return pltpu.make_async_copy(
+            act.at[r], agath.at[r, pl.ds(pl.multiple_of(p * n, n), n)], loc_sem.at[1, r]
+        )
+
+    def rows_of(q):
+        return pl.ds(pl.multiple_of(q * n, n), n)
+
+    def x_send(r, j):
+        return remote(act.at[r], agath.at[r, rows_of(p)], xs.at[r, j], xr.at[r, x], "param", xpeer(j))
+
+    def x_recv(r, j):
+        q = xpeer(j)
+        return remote(act.at[r], agath.at[r, rows_of(q)], xs.at[r, j], xr.at[r, q // 2], "param", q)
+
+    def b_send(r):
+        return remote(act.at[r], agath.at[r, rows_of(p)], bs.at[r], br.at[r], "param", sib)
+
+    def b_recv(r):
+        return remote(act.at[r], agath.at[r, rows_of(sib)], bs.at[r], br.at[r], "param", sib)
+
+    def f_send(r, j):
+        q = xpeer(j)
+        return remote(
+            agath.at[r, rows_of(q)], agath.at[r, rows_of(q)], fs.at[r, j], fr.at[r, j], "param", sib
+        )
+
+    def f_recv(r, j):
+        q = lax.rem(x + j, X) * 2 + (1 - c)
+        return remote(
+            agath.at[r, rows_of(q)], agath.at[r, rows_of(q)], fs.at[r, j], fr.at[r, j], "param", sib
+        )
+
+    def chunk(q):
+        return pl.ds(pl.multiple_of(q * dc, dc), dc)
+
+    def z_send(i, k):
+        q = lax.rem(z + k, Z)
+        return remote(sbuf.at[i, chunk(q)], rbuf.at[z, i], zs.at[i, k], zr.at[i, z], "walker", q)
+
+    def z_recv(i, k):
+        q = lax.rem(z + k, Z)
+        return remote(sbuf.at[i, chunk(q)], rbuf.at[q, i], zs.at[i, k], zr.at[i, q], "walker", q)
+
+    def p_send(j):
+        q = lax.rem(p + j, PP)
+        return remote(prev.at[chunk(z)], stored.at[p], ps.at[j], pr.at[p], "param", q)
+
+    def p_recv(j):
+        q = lax.rem(p + j, PP)
+        return remote(prev.at[chunk(z)], stored.at[q], ps.at[j], pr.at[q], "param", q)
+
+    def g_send(j):
+        q = lax.rem(p + j, PP)
+        return remote(gsum, gred.at[p], gs.at[j], gr.at[p], "param", q)
+
+    def g_recv(j):
+        q = lax.rem(p + j, PP)
+        return remote(gsum, gred.at[q], gs.at[j], gr.at[q], "param", q)
+
+    def h_send(k):
+        q = lax.rem(z + k, Z)
+        return remote(zred.at[z], zred.at[z], hs.at[k], hr.at[z], "walker", q)
+
+    def h_recv(k):
+        q = lax.rem(z + k, Z)
+        return remote(zred.at[q], zred.at[q], hs.at[k], hr.at[q], "walker", q)
+
+    def d_send(k):
+        q = lax.rem(z + k, Z)
+        return remote(dscr.at[chunk(z)], dscr.at[chunk(z)], ds.at[k], dr.at[z], "walker", q)
+
+    def d_recv(k):
+        q = lax.rem(z + k, Z)
+        return remote(dscr.at[chunk(q)], dscr.at[chunk(q)], ds.at[k], dr.at[q], "walker", q)
+
+    def e_send(k):
+        q = lax.rem(z + k, Z)
+        return remote(packed, ebuf.at[z], es.at[k], er.at[z], "walker", q)
+
+    def e_recv(k):
+        q = lax.rem(z + k, Z)
+        return remote(packed, ebuf.at[q], es.at[k], er.at[q], "walker", q)
+
+    barrier = pltpu.get_barrier_semaphore()
+    for j in range(1, PP):
+        pl.semaphore_signal(barrier, inc=1, device_id={"param": lax.rem(p + j, PP)}, device_id_type=MESH)
+    for k in range(1, Z):
+        pl.semaphore_signal(barrier, inc=1, device_id={"walker": lax.rem(z + k, Z)}, device_id_type=MESH)
+
+    def start_local(r, _):
+        cot_copy(r).start()
+        act_copy(r).start()
+        return 0
+
+    lax.fori_loop(0, R, start_local, 0)
+    pl.semaphore_wait(barrier, PP + Z - 2)
+
+    def start_sends(r, _):
+        for j in range(1, X):
+            x_send(r, j).start()
+        b_send(r).start()
+        return 0
+
+    lax.fori_loop(0, R, start_sends, 0)
+    for k in range(1, Z):
+        e_send(k).start()
+    for j in range(1, PP):
+        p_send(j).start()
+
+    def forward(r):
+        for j in range(1, X):
+            x_recv(r, j).wait_recv()
+            f_send(r, j).start()
+
+    def grads_of(r):
+        cot_copy(r).wait()
+        act_copy(r).wait()
+        b_recv(r).wait_recv()
+        for j in range(1, X):
+            f_recv(r, j).wait_recv()
+        flipped = jnp.dot(cbuf[r], agath[r], preferred_element_type=F32)
+        return flipped.T
+
+    def send_row(i):
+        rbuf[z, i] = sbuf[i, chunk(z), :]
+        for k in range(1, Z):
+            z_send(i, k).start()
+
+    def first():
+        g = grads_of(0)
+        high = g.astype(BF16)
+        low = (g - high.astype(F32)).astype(BF16)
+        sbuf[0] = high
+        sbuf[R] = low
+        run[...] = high.astype(F32) + low.astype(F32)
+        send_row(0)
+        send_row(R)
+
+    def inverse(r):
+        return 1.0 / jnp.asarray(r, F32)
+
+    def later(r):
+        g = grads_of(r)
+        middle = run[...] * inverse(r)
+        step = (g - middle).astype(BF16)
+        sbuf[r] = step
+        run[...] += middle + step.astype(F32)
+        send_row(r)
+
+    forward(0)
+    forward(1)
+    first()
+
+    def body(r, _):
+        forward(r)
+        later(r - 1)
+        return 0
+
+    lax.fori_loop(2, R, body, 0)
+    later(R - 1)
+
+    for j in range(1, PP):
+        p_recv(j).wait_recv()
+    stored[p] = prev[chunk(z), :]
+    mine = order[:, pl.ds(pl.multiple_of(p * O, O), O)]
+    acc = jnp.zeros((3 * dc, O), F32)
+    for q in range(PP):
+        hot = (lax.broadcasted_iota(jnp.int32, (O, O), 0) + q * O == mine).astype(F32).astype(BF16)
+        s = stored[q]
+        s1 = s.astype(BF16)
+        rest = s - s1.astype(F32)
+        s2 = rest.astype(BF16)
+        s3 = (rest - s2.astype(F32)).astype(BF16)
+        acc += jnp.dot(jnp.concatenate([s1, s2, s3], axis=0), hot, preferred_element_type=F32)
+    alig[...] = acc[:dc] + (acc[dc : 2 * dc] + acc[2 * dc :])
+
+    for k in range(1, Z):
+        e_recv(k).wait_recv()
+    ebuf[z] = packed[...]
+    lane = lax.broadcasted_iota(jnp.int32, (R, 128), 1)
+    energy_sum = jnp.zeros((1, 1), F32)
+    for q in range(Z):
+        energy_sum += jnp.sum(ebuf[q, R : R + 1, :], axis=1, keepdims=True)
+    energy_mean = energy_sum / W
+    for q in range(Z):
+        ids = ebuf[q, 0:R, :]
+        picked = jnp.zeros((R, 128), F32)
+        for s in range(Z):
+            hit = (ids == (lane + s * R).astype(F32)) & (lane < R)
+            picked += jnp.where(hit, ebuf[s, R : R + 1, :], 0.0)
+        value = jnp.sum(picked, axis=1, keepdims=True) - energy_mean
+        esort[q * R : (q + 1) * R, :] = jnp.broadcast_to(value, (R, 128))
+
+    for k in range(1, Z):
+        z_recv(0, k).wait_recv()
+        z_recv(R, k).wait_recv()
+
+    def put(q, r, g):
+        for h in range(halves):
+            cent[h, pl.ds(pl.multiple_of((q * R + r) * dc, dc), dc), :] = g[:, h * 128 : (h + 1) * 128]
+
+    for q in range(Z):
+        g = rbuf[q, 0].astype(F32) + rbuf[q, R].astype(F32)
+        runs[q] = g
+        put(q, 0, g)
+
+    def rebuild(r, _):
+        for k in range(1, Z):
+            z_recv(r, k).wait_recv()
+        for q in range(Z):
+            middle = runs[q] * inverse(r)
+            g = middle + rbuf[q, r].astype(F32)
+            put(q, r, g)
+            runs[q] += g
+        return 0
+
+    lax.fori_loop(1, R, rebuild, 0)
+    acc = runs[0]
+    for q in range(1, Z):
+        acc += runs[q]
+    mean_ref[...] = acc * (1.0 / W)
+
+    def gram_step(i, carry):
+        gram, proj = carry
+        parts = []
+        for u in range(4):
+            d = i * 4 + u
+            row = jnp.concatenate(
+                [cent[h, pl.ds(d, W, stride=dc), :] for h in range(halves)], axis=1
+            )
+            row = row - mean_ref[pl.ds(d, 1), :]
+            proj = proj + row * alig[pl.ds(d, 1), :]
+            parts.append(row.astype(BF16))
+        wide = jnp.concatenate(parts, axis=1)
+        gram = gram + lax.dot_general(
+            wide, wide, (((1,), (1,)), ((), ())), preferred_element_type=F32
+        )
+        return gram, proj
+
+    gram, proj = lax.fori_loop(
+        0, dc // 4, gram_step, (jnp.zeros((W, W), F32), jnp.zeros((W, O), F32))
+    )
+    gsum[...] = jnp.zeros((W, L), F32)
+    gsum[:, 0:W] = gram
+    gsum[:, W : W + 1] = jnp.sum(proj, axis=1, keepdims=True)
+    for j in range(1, PP):
+        g_send(j).start()
+    gred[p] = gsum[...]
+    for j in range(1, PP):
+        g_recv(j).wait_recv()
+    acc = gred[0]
+    for q in range(1, PP):
+        acc += gred[q]
+    zred[z] = acc
+    for k in range(1, Z):
+        h_send(k).start()
+    for k in range(1, Z):
+        h_recv(k).wait_recv()
+    acc = zred[0]
+    for q in range(1, Z):
+        acc += zred[q]
+
+    sub = lax.broadcasted_iota(jnp.int32, (W, L), 0)
+    col = lax.broadcasted_iota(jnp.int32, (W, L), 1)
+    damp = jnp.where(sub == col, 0.002, 0.0) + 1.0 / W
+    zeta = esort[:, 0:1] - 0.9 * acc[:, W : W + 1]
+    m = jnp.where(col == W, zeta, acc + damp)
+    for k in range(W):
+        pivot_row = m[k : k + 1, :]
+        pivot_row = pivot_row / pivot_row[:, k : k + 1]
+        m = jnp.where(sub == k, pivot_row, m - m[:, k : k + 1] * pivot_row)
+    solved = jnp.broadcast_to(m[:, W : W + 1], (W, 128))
+    csol[...] = solved
+    sub = lax.broadcasted_iota(jnp.int32, (W, 128), 0)
+    col = lax.broadcasted_iota(jnp.int32, (W, 128), 1)
+    coef_out[...] = jnp.sum(jnp.where(sub == col + z * R, solved, 0.0), axis=0, keepdims=True)
+
+    for h in range(halves):
+        cols = slice(h * 128, (h + 1) * 128)
+        mean_half = mean_ref[:, cols]
+
+        def add(w, acc):
+            part = cent[h, pl.ds(pl.multiple_of(w * dc, dc), dc), :] - mean_half
+            return acc + csol[pl.ds(w, 1), :] * part
+
+        acc = lax.fori_loop(0, W, add, jnp.zeros((dc, 128), F32), unroll=4)
+        dscr[chunk(z), cols] = acc + 0.9 * alig[:, cols]
+    for k in range(1, Z):
+        d_send(k).start()
+    for k in range(1, Z):
+        d_recv(k).wait_recv()
+    value = dscr[...]
+    dir_out[...] = value
+    w_out[...] = weights[...] - 0.05 * value
+
+    def drain(r, _):
+        for j in range(1, X):
+            x_send(r, j).wait_send()
+            f_send(r, j).wait_send()
+        b_send(r).wait_send()
+        return 0
+
+    lax.fori_loop(0, R, drain, 0)
+
+    def drain_rows(i, _):
+        for k in range(1, Z):
+            z_send(i, k).wait_send()
+        return 0
+
+    lax.fori_loop(0, R + 1, drain_rows, 0)
+    for j in range(1, PP):
+        p_send(j).wait_send()
+        g_send(j).wait_send()
+    for k in range(1, Z):
+        e_send(k).wait_send()
+        h_send(k).wait_send()
+        d_send(k).wait_send()
+
+
+def fused_shards(
+    activations, cotangents, local_energy, walker_ids, prev_direction, column_order, weights
+):
+    R, n, D = activations.shape
+    O, N = cotangents.shape[1:]
+    Z = lax.axis_size("walker")
+    PP = lax.axis_size("param")
+    X = PP // 2
+    W = R * Z
+    dc = D // Z
+    L = -(-(W + 1) // 128) * 128
+    rp = -(-(R + 1) // 8) * 8
+    packed = jnp.zeros((rp, 128), F32)
+    packed = packed.at[:R, :].set(jnp.broadcast_to(walker_ids.astype(F32)[:, None], (R, 128)))
+    packed = packed.at[R, :R].set(local_energy)
+    vmem = pl.BlockSpec(memory_space=pltpu.VMEM)
+    hbm = pl.BlockSpec(memory_space=pl.ANY)
+    dma = pltpu.SemaphoreType.DMA
+    direction, new_weights, coef = pl.pallas_call(
+        functools.partial(kernel, Z=Z, PP=PP),
+        out_shape=(
+            jax.ShapeDtypeStruct((D, O), F32),
+            jax.ShapeDtypeStruct((D, O), F32),
+            jax.ShapeDtypeStruct((1, 128), F32),
+        ),
+        in_specs=[hbm, hbm, vmem, vmem, vmem, vmem],
+        out_specs=(vmem, vmem, vmem),
+        scratch_shapes=[
+            pltpu.VMEM((R, N, D), BF16),
+            pltpu.VMEM((R, O, N), BF16),
+            pltpu.VMEM((R + 1, D, O), BF16),
+            pltpu.VMEM((Z, R + 1, dc, O), BF16),
+            pltpu.VMEM((D, O), F32),
+            pltpu.VMEM((Z, dc, O), F32),
+            pltpu.VMEM((dc, O), F32),
+            pltpu.VMEM((O // 128, W * dc, 128), F32),
+            pltpu.VMEM((PP, dc, O), F32),
+            pltpu.VMEM((dc, O), F32),
+            pltpu.VMEM((dc, O), F32),
+            pltpu.VMEM((PP, W, L), F32),
+            pltpu.VMEM((Z, W, L), F32),
+            pltpu.VMEM((W, L), F32),
+            pltpu.VMEM((D, O), F32),
+            pltpu.VMEM((Z, rp, 128), F32),
+            pltpu.VMEM((W, 128), F32),
+            pltpu.VMEM((W, 128), F32),
+            dma((2, R)),
+            dma((R, X)), dma((R, X)),
+            dma((R,)), dma((R,)),
+            dma((R, X)), dma((R, X)),
+            dma((R + 1, Z)), dma((R + 1, Z)),
+            dma((PP,)), dma((PP,)),
+            dma((PP,)), dma((PP,)),
+            dma((Z,)), dma((Z,)),
+            dma((Z,)), dma((Z,)),
+            dma((Z,)), dma((Z,)),
+        ],
+        compiler_params=pltpu.CompilerParams(
+            collective_id=0, has_side_effects=True, vmem_limit_bytes=48 * 1024 * 1024
+        ),
+        cost_estimate=pl.CostEstimate(
+            flops=2 * R * D * O * N, bytes_accessed=2 * R * N * (D + O), transcendentals=0
+        ),
+    )(activations, cotangents, prev_direction, column_order.reshape(1, -1), weights, packed)
+    return (direction, new_weights, coef[0, :R])
+
+
+def shards(*args):
+    R, n, D = args[0].shape
+    O = args[1].shape[1]
+    Z = lax.axis_size("walker")
+    fits = O % 128 == 0 and D % (16 * Z) == 0 and R * Z <= 120 and R >= 3 and n % 16 == 0
+    if fits and lax.axis_size("param") % 2 == 0:
+        return fused_shards(*args)
+    return plain_shards(*args)
+
+
 def solution(mesh):
     in_specs = (
         P(("group", "walker"), "param", None),

time: 369 us -> 83.9 us (0.23)
  waiting for transfers between devices: 250 us -> 0 us
  Pallas kernels: 0 us -> 75.6 us
  blocking collectives: 40 us -> 0 us
  local copies, waits for them, and re-layouts: 26.4 us -> 6.73 us
  other arithmetic: 19.9 us -> 0.66 us
  matrix products: 16.6 us -> 0 us
  between operations: 15.3 us -> 0.65 us
    all_gather x3 -> x0, waiting for transfers between devices: 187 us -> none  [the longest x1 137 us: shards(): lax.all_gather(centered, 'walker', axis=0, tiled=True)]
    pallas_call x0 -> x1, Pallas kernels: none -> 75.6 us  [fused_shards(): pl.pallas_call(functools.partial(kernel, Z=Z, PP=PP), out_shape=(jax.Shap...]
    psum x2 -> x0, waiting for transfers between devices: 63.1 us -> none  [the longest x1 33.5 us: shards(): update_total = lax.psum(update_part, 'walker')]
    unnamed x2 -> x0, blocking collectives: 19.6 us -> none
    dot_general x4 -> x0, matrix products: 16.3 us -> none  [the longest x1 6.46 us: shards(): jnp.einsum('wnd,won->wdo', lax.all_gather(activations, 'param', axis=1, t...]
    unnamed x32 -> x10, local copies, waits for them, and re-layouts: 19.2 us -> 5.39 us
    all_gather x1 -> x0, blocking collectives: 13.1 us -> none  [shards(): lax.all_gather(gram_mine, 'walker', axis=0, tiled=True)]
    another operation x5 -> x0, other arithmetic: 9.37 us -> none  [the longest x3 5.05 us: solve_system(): factor = jnp.linalg.cholesky(system)]
  transfers between devices with their start and end apart: 5 -> 0, of which waited for: 4 -> 0; matrix products, arithmetic and copies ran while one was open for 7% -> 0% of each run, Pallas kernels for 0% -> 0%
where the time goes in v1:
time: 83.9 us; the launch traced here: 83.7 us
  Pallas kernels  75.6 us (90%)
  local copies, waits for them, and re-layouts  6.73 us (8%)
    pallas_call x1, Pallas kernels, fused_shards(): pl.pallas_call(functools.partial(kernel, Z=Z, PP=PP), out_shape=(jax.Shap...  75.6 us
    unnamed x10, local copies, waits for them, and re-layouts  5.39 us

profile of v1, /device:TPU:0, one launch (start us, length us, event | category | flops | bytes accessed | tf_op | source)
XLA Modules:
  0.0 83.7 jit_solution(12285876927607333490)
XLA Ops:
  0.6 0.7 convert_element_type.3
  1.3 0.1 scatter.13
  1.4 0.7 scatter.14.packed
  2.1 0.0 copy-start
  2.1 1.4 %copy-done = bf16[12,256,256]{2,1,0:T(8,128)(2,1)S(1)} copy-done((bf16[12,256,256]{2,1,0:T(8,128)(2,1)S(1)}, bf16[12,256,256]{2,1,0:T(8,128)(2,1)}, u32[]{:S(2)}) %copy-start) | copy-done | bytes 1572888
  3.5 0.0 copy-start.1
  3.5 0.9 %copy-done.1 = f32[256,256]{1,0:T(8,128)S(1)} copy-done((f32[256,256]{1,0:T(8,128)S(1)}, f32[256,256]{1,0:T(8,128)}, u32[]{:S(2)}) %copy-start.1) | copy-done | bytes 262168
  4.5 0.0 copy-start.2
  4.5 0.9 %copy-done.2 = f32[256,256]{1,0:T(8,128)S(1)} copy-done((f32[256,256]{1,0:T(8,128)S(1)}, f32[256,256]{1,0:T(8,128)}, u32[]{:S(2)}) %copy-start.2) | copy-done | bytes 262168
  5.4 0.0 copy-start.3
  5.4 0.7 copy-done.3
  6.1 75.6 %shard_map.94 = (f32[256,256]{1,0:T(8,128)S(1)}, f32[256,256]{1,0:T(8,128)S(1)}, f32[1,128]{1,0:T(1,128)S(1)}) custom-call(bf16[12,256,256]{2,1,0:T(8,128)(2,1)S(1)} %copy-done, bf16[12,256,1024]{2,1,0:T(8,128)(2,1)} %cot.1, f32[256,256]{1,0:T(8,128)S(1)} %copy-done.1, s32[1,1024]{1,0:T(1,128)S(1)} %bitcast.4, f32[256,256]{1,0:T(8,128)S(1)} %copy-done.2, ...), custom_call_target="tpu_custom_call" | custom-call | flops 1610612736 | bytes 12582912 | tf_op jit(solution)/shard_map/pallas_call | solution.py:445
  81.8 0.5 slice_bitcast_fusion
  82.3 0.7 copy.13
  83.0 0.7 copy.14
  (1 shorter events, 0.0 us)
Async XLA Ops:
  2.1 1.4 %copy-start = (bf16[12,256,256]{2,1,0:T(8,128)(2,1)S(1)}, bf16[12,256,256]{2,1,0:T(8,128)(2,1)}, u32[]{:S(2)}) copy-start(bf16[12,256,256]{2,1,0:T(8,128)(2,1)} %act.1) | copy-start | bytes 4718596
  3.5 0.9 %copy-start.1 = (f32[256,256]{1,0:T(8,128)S(1)}, f32[256,256]{1,0:T(8,128)}, u32[]{:S(2)}) copy-start(f32[256,256]{1,0:T(8,128)} %prev.1) | copy-start | bytes 786436
  4.5 0.9 %copy-start.2 = (f32[256,256]{1,0:T(8,128)S(1)}, f32[256,256]{1,0:T(8,128)}, u32[]{:S(2)}) copy-start(f32[256,256]{1,0:T(8,128)} %weights.1) | copy-start | bytes 786436
  5.4 0.7 copy-start.3

commit v2 on v1

--- a/solution.py
+++ b/solution.py
@@ -10,6 +10,7 @@
 F32 = jnp.float32
 BF16 = jnp.bfloat16
 MESH = pl.DeviceIdType.MESH
+WINDOW = 2
 
 
 def solve_system(system, zeta):
@@ -72,11 +73,11 @@
 
 
 def kernel(
-    act, cot, prev, order, weights, packed,
-    dir_out, w_out, coef_out,
+    act, cot, prev_in, order_in, energy_in, ids_in,
+    dir_out, coef_out,
     agath, cbuf, sbuf, rbuf, run, runs, total, cent, stored, alig, mean_ref,
-    gred, zred, gsum, dscr, ebuf, esort, csol,
-    loc_sem, xs, xr, bs, br, fs, fr, zs, zr, ps, pr, gs, gr, hs, hr, ds, dr, es, er,
+    gred, zred, gsum, dscr, ebuf, esort, csol, prev, order, energy, ids_ref, packed,
+    loc_sem, in_sem, xs, xr, bs, br, fs, fr, zs, zr, ps, pr, pbs, pbr, pfs, pfr, gs, gr, hs, hr, ds, dr, es, er,
     *, Z, PP,
 ):
     R, n, D = act.shape
@@ -85,6 +86,7 @@
     X = PP // 2
     dc = D // Z
     L = gsum.shape[1]
+    fold = gsum.shape[0] != W
     halves = O // 128
     z = lax.axis_index("walker")
     p = lax.axis_index("param")
@@ -149,12 +151,25 @@
         return remote(sbuf.at[i, chunk(q)], rbuf.at[q, i], zs.at[i, k], zr.at[i, q], "walker", q)
 
     def p_send(j):
-        q = lax.rem(p + j, PP)
-        return remote(prev.at[chunk(z)], stored.at[p], ps.at[j], pr.at[p], "param", q)
+        return remote(prev.at[chunk(z)], stored.at[p], ps.at[j], pr.at[x], "param", xpeer(j))
 
     def p_recv(j):
-        q = lax.rem(p + j, PP)
-        return remote(prev.at[chunk(z)], stored.at[q], ps.at[j], pr.at[q], "param", q)
+        q = xpeer(j)
+        return remote(prev.at[chunk(z)], stored.at[q], ps.at[j], pr.at[q // 2], "param", q)
+
+    def pb_send():
+        return remote(prev.at[chunk(z)], stored.at[p], pbs.at[0], pbr.at[0], "param", sib)
+
+    def pb_recv():
+        return remote(prev.at[chunk(z)], stored.at[sib], pbs.at[0], pbr.at[0], "param", sib)
+
+    def pf_send(j):
+        q = xpeer(j)
+        return remote(stored.at[q], stored.at[q], pfs.at[j], pfr.at[j], "param", sib)
+
+    def pf_recv(j):
+        q = lax.rem(x + j, X) * 2 + (1 - c)
+        return remote(stored.at[q], stored.at[q], pfs.at[j], pfr.at[j], "param", sib)
 
     def g_send(j):
         q = lax.rem(p + j, PP)
@@ -193,6 +208,15 @@
         pl.semaphore_signal(barrier, inc=1, device_id={"param": lax.rem(p + j, PP)}, device_id_type=MESH)
     for k in range(1, Z):
         pl.semaphore_signal(barrier, inc=1, device_id={"walker": lax.rem(z + k, Z)}, device_id_type=MESH)
+
+    inputs = [
+        pltpu.make_async_copy(src, dst, in_sem.at[i])
+        for i, (src, dst) in enumerate(
+            ((prev_in, prev), (order_in, order), (energy_in, energy), (ids_in, ids_ref))
+        )
+    ]
+    for copy in inputs:
+        copy.start()
 
     def start_local(r, _):
         cot_copy(r).start()
@@ -202,22 +226,42 @@
     lax.fori_loop(0, R, start_local, 0)
     pl.semaphore_wait(barrier, PP + Z - 2)
 
-    def start_sends(r, _):
+    def start_x(r):
         for j in range(1, X):
             x_send(r, j).start()
+
+    for r in range(WINDOW):
+        start_x(r)
+
+    def start_b(r, _):
         b_send(r).start()
         return 0
 
-    lax.fori_loop(0, R, start_sends, 0)
+    lax.fori_loop(0, R, start_b, 0)
+    for copy in inputs:
+        copy.wait()
+    pb_send().start()
+    packed[...] = jnp.zeros(packed.shape, F32)
+    eye = lax.broadcasted_iota(jnp.int32, (R, R), 0) == lax.broadcasted_iota(jnp.int32, (R, R), 1)
+    id_column = jnp.sum(jnp.where(eye, ids_ref[...].astype(F32), 0.0), axis=1, keepdims=True)
+    packed[0:R, :] = jnp.broadcast_to(id_column, (R, 128))
+    packed[R : R + 1, 0:R] = energy[...]
     for k in range(1, Z):
         e_send(k).start()
-    for j in range(1, PP):
-        p_send(j).start()
-
-    def forward(r):
+
+    def forward(r, last=False):
         for j in range(1, X):
             x_recv(r, j).wait_recv()
             f_send(r, j).start()
+        for j in range(1, X):
+            x_send(r, j).wait_send()
+        if last:
+            return
+        if isinstance(r, int):
+            if r + WINDOW < R:
+                start_x(r + WINDOW)
+        else:
+            pl.when(r + WINDOW < R)(lambda: start_x(r + WINDOW))
 
     def grads_of(r):
         cot_copy(r).wait()
@@ -263,12 +307,20 @@
         later(r - 1)
         return 0
 
-    lax.fori_loop(2, R, body, 0)
+    lax.fori_loop(2, R - 1, body, 0)
+    forward(R - 1, last=True)
+    for j in range(1, X):
+        p_send(j).start()
+    later(R - 2)
     later(R - 1)
 
-    for j in range(1, PP):
+    stored[p] = prev[chunk(z), :]
+    pb_recv().wait_recv()
+    for j in range(1, X):
         p_recv(j).wait_recv()
-    stored[p] = prev[chunk(z), :]
+        pf_send(j).start()
+    for j in range(1, X):
+        pf_recv(j).wait_recv()
     mine = order[:, pl.ds(pl.multiple_of(p * O, O), O)]
     acc = jnp.zeros((3 * dc, O), F32)
     for q in range(PP):
@@ -347,9 +399,13 @@
     gram, proj = lax.fori_loop(
         0, dc // 4, gram_step, (jnp.zeros((W, W), F32), jnp.zeros((W, O), F32))
     )
-    gsum[...] = jnp.zeros((W, L), F32)
-    gsum[:, 0:W] = gram
-    gsum[:, W : W + 1] = jnp.sum(proj, axis=1, keepdims=True)
+    whole = jnp.concatenate(
+        [gram, jnp.sum(proj, axis=1, keepdims=True), jnp.zeros((W, L - W - 1), F32)], axis=1
+    )
+    if fold:
+        gsum[...] = whole[: W // 2] + pltpu.roll(whole[W // 2 :], L // 2, 1)
+    else:
+        gsum[...] = whole
     for j in range(1, PP):
         g_send(j).start()
     gred[p] = gsum[...]
@@ -366,16 +422,24 @@
     acc = zred[0]
     for q in range(1, Z):
         acc += zred[q]
+    if fold:
+        acc = jnp.concatenate([acc, pltpu.roll(acc, L // 2, 1)], axis=0)
 
     sub = lax.broadcasted_iota(jnp.int32, (W, L), 0)
     col = lax.broadcasted_iota(jnp.int32, (W, L), 1)
     damp = jnp.where(sub == col, 0.002, 0.0) + 1.0 / W
     zeta = esort[:, 0:1] - 0.9 * acc[:, W : W + 1]
     m = jnp.where(col == W, zeta, acc + damp)
-    for k in range(W):
-        pivot_row = m[k : k + 1, :]
-        pivot_row = pivot_row / pivot_row[:, k : k + 1]
-        m = jnp.where(sub == k, pivot_row, m - m[:, k : k + 1] * pivot_row)
+    for k in range(0, W, 2):
+        r0, r1 = m[k : k + 1, :], m[k + 1 : k + 2, :]
+        c0, c1 = m[:, k : k + 1], m[:, k + 1 : k + 2]
+        up, low = r0[:, k + 1 : k + 2], r1[:, k : k + 1]
+        inv0 = 1.0 / r0[:, k : k + 1]
+        ratio = up * inv0
+        inv1 = 1.0 / (r1[:, k + 1 : k + 2] - low * ratio)
+        p1 = (r1 - (low * inv0) * r0) * inv1
+        p0 = r0 * inv0 - ratio * p1
+        m = jnp.where(sub == k, p0, jnp.where(sub == k + 1, p1, m - c0 * p0 - c1 * p1))
     solved = jnp.broadcast_to(m[:, W : W + 1], (W, 128))
     csol[...] = solved
     sub = lax.broadcasted_iota(jnp.int32, (W, 128), 0)
@@ -396,13 +460,10 @@
         d_send(k).start()
     for k in range(1, Z):
         d_recv(k).wait_recv()
-    value = dscr[...]
-    dir_out[...] = value
-    w_out[...] = weights[...] - 0.05 * value
+    dir_out[...] = dscr[...]
 
     def drain(r, _):
         for j in range(1, X):
-            x_send(r, j).wait_send()
             f_send(r, j).wait_send()
         b_send(r).wait_send()
         return 0
@@ -416,8 +477,11 @@
 
     lax.fori_loop(0, R + 1, drain_rows, 0)
     for j in range(1, PP):
+        g_send(j).wait_send()
+    pb_send().wait_send()
+    for j in range(1, X):
         p_send(j).wait_send()
-        g_send(j).wait_send()
+        pf_send(j).wait_send()
     for k in range(1, Z):
         e_send(k).wait_send()
         h_send(k).wait_send()
@@ -436,21 +500,18 @@
     dc = D // Z
     L = -(-(W + 1) // 128) * 128
     rp = -(-(R + 1) // 8) * 8
-    packed = jnp.zeros((rp, 128), F32)
-    packed = packed.at[:R, :].set(jnp.broadcast_to(walker_ids.astype(F32)[:, None], (R, 128)))
-    packed = packed.at[R, :R].set(local_energy)
+    grows = W // 2 if L == 128 and W + 1 <= 64 and W % 16 == 0 else W
     vmem = pl.BlockSpec(memory_space=pltpu.VMEM)
-    hbm = pl.BlockSpec(memory_space=pl.ANY)
+    hbm = pl.BlockSpec(memory_space=pltpu.HBM)
     dma = pltpu.SemaphoreType.DMA
-    direction, new_weights, coef = pl.pallas_call(
+    direction, coef = pl.pallas_call(
         functools.partial(kernel, Z=Z, PP=PP),
         out_shape=(
             jax.ShapeDtypeStruct((D, O), F32),
-            jax.ShapeDtypeStruct((D, O), F32),
             jax.ShapeDtypeStruct((1, 128), F32),
         ),
-        in_specs=[hbm, hbm, vmem, vmem, vmem, vmem],
-        out_specs=(vmem, vmem, vmem),
+        in_specs=[hbm] * 6,
+        out_specs=(vmem, vmem),
         scratch_shapes=[
             pltpu.VMEM((R, N, D), BF16),
             pltpu.VMEM((R, O, N), BF16),
@@ -463,39 +524,67 @@
             pltpu.VMEM((PP, dc, O), F32),
             pltpu.VMEM((dc, O), F32),
             pltpu.VMEM((dc, O), F32),
-            pltpu.VMEM((PP, W, L), F32),
-            pltpu.VMEM((Z, W, L), F32),
-            pltpu.VMEM((W, L), F32),
+            pltpu.VMEM((PP, grows, L), F32),
+            pltpu.VMEM((Z, grows, L), F32),
+            pltpu.VMEM((grows, L), F32),
             pltpu.VMEM((D, O), F32),
             pltpu.VMEM((Z, rp, 128), F32),
             pltpu.VMEM((W, 128), F32),
             pltpu.VMEM((W, 128), F32),
+            pltpu.VMEM((D, O), F32),
+            pltpu.VMEM((1, O * PP), jnp.int32),
+            pltpu.VMEM((1, R), F32),
+            pltpu.VMEM((1, R), jnp.int32),
+            pltpu.VMEM((rp, 128), F32),
             dma((2, R)),
+            dma((4,)),
             dma((R, X)), dma((R, X)),
             dma((R,)), dma((R,)),
             dma((R, X)), dma((R, X)),
             dma((R + 1, Z)), dma((R + 1, Z)),
-            dma((PP,)), dma((PP,)),
+            dma((X,)), dma((X,)),
+            dma((1,)), dma((1,)),
+            dma((X,)), dma((X,)),
             dma((PP,)), dma((PP,)),
             dma((Z,)), dma((Z,)),
             dma((Z,)), dma((Z,)),
             dma((Z,)), dma((Z,)),
         ],
         compiler_params=pltpu.CompilerParams(
-            collective_id=0, has_side_effects=True, vmem_limit_bytes=48 * 1024 * 1024
+            collective_id=0, has_side_effects=True, vmem_limit_bytes=60 * 1024 * 1024
         ),
         cost_estimate=pl.CostEstimate(
             flops=2 * R * D * O * N, bytes_accessed=2 * R * N * (D + O), transcendentals=0
         ),
-    )(activations, cotangents, prev_direction, column_order.reshape(1, -1), weights, packed)
-    return (direction, new_weights, coef[0, :R])
+    )(
+        activations, cotangents, prev_direction, column_order.reshape(1, -1),
+        local_energy.reshape(1, -1), walker_ids.reshape(1, -1),
+    )
+
+    def finish(d_ref, c_ref, w_ref, dir_ref, new_ref, mine_ref):
+        value = d_ref[...]
+        dir_ref[...] = value
+        new_ref[...] = w_ref[...] - 0.05 * value
+        mine_ref[...] = c_ref[:, 0:R]
+
+    direction, new_weights, mine = pl.pallas_call(
+        finish,
+        out_shape=(
+            jax.ShapeDtypeStruct((D, O), F32),
+            jax.ShapeDtypeStruct((D, O), F32),
+            jax.ShapeDtypeStruct((1, R), F32),
+        ),
+        in_specs=[vmem] * 3,
+        out_specs=(vmem, vmem, vmem),
+    )(direction, coef, weights)
+    return (direction, new_weights, mine.reshape(-1))
 
 
 def shards(*args):
     R, n, D = args[0].shape
     O = args[1].shape[1]
     Z = lax.axis_size("walker")
-    fits = O % 128 == 0 and D % (16 * Z) == 0 and R * Z <= 120 and R >= 3 and n % 16 == 0
+    fits = O % 128 == 0 and D % (16 * Z) == 0 and R * Z <= 120 and R >= 4 and R * Z % 2 == 0 and n % 16 == 0
     if fits and lax.axis_size("param") % 2 == 0:
         return fused_shards(*args)
     return plain_shards(*args)

time: 83.9 us -> 81.8 us (0.975)
  local copies, waits for them, and re-layouts: 6.73 us -> 0 us
  Pallas kernels: 75.6 us -> 81 us
    unnamed x10 -> x0, local copies, waits for them, and re-layouts: 5.39 us -> none
    pallas_call x1, Pallas kernels: 75.6 us -> 79.2 us  [fused_shards(): pl.pallas_call(functools.partial(kernel, Z=Z, PP=PP), out_shape=(jax.Shap...]
    pallas_call x0 -> x1, Pallas kernels: none -> 1.86 us  [fused_shards(): pl.pallas_call(finish, out_shape=(jax.ShapeDtypeStruct((D, O), F32), jax....]
where the time goes in v2:
time: 81.8 us; the launch traced here: 81.7 us
  Pallas kernels  81 us (99%)
    pallas_call x1, Pallas kernels, fused_shards(): pl.pallas_call(functools.partial(kernel, Z=Z, PP=PP), out_shape=(jax.Shap...  79.2 us
    pallas_call x1, Pallas kernels, fused_shards(): pl.pallas_call(finish, out_shape=(jax.ShapeDtypeStruct((D, O), F32), jax....  1.86 us

profile of v2, /device:TPU:0, one launch (start us, length us, event | category | flops | bytes accessed | tf_op | source)
XLA Modules:
  0.0 81.7 jit_solution(6814532492671504699)
XLA Ops:
  0.6 79.2 %shard_map.94 = (f32[256,256]{1,0:T(8,128)}, f32[1,128]{1,0:T(1,128)}) custom-call(bf16[12,256,256]{2,1,0:T(8,128)(2,1)} %act.1, bf16[12,256,1024]{2,1,0:T(8,128)(2,1)} %cot.1, f32[256,256]{1,0:T(8,128)} %prev_in.1, s32[1,1024]{1,0:T(1,128)} %bitcast.4, f32[1,12]{1,0:T(1,128)} %bitcast.5, s32[1,12]{1,0:T(1,128)} %bitcast.6), custom_call_target="tpu_custom_call" | custom-call | flops 1610612736 | bytes 12582912 | tf_op jit(solution)/shard_map/pallas_call | solution.py:507
  79.8 1.9 %shard_map.95 = (f32[256,256]{1,0:T(8,128)}, f32[256,256]{1,0:T(8,128)}, f32[1,12]{1,0:T(1,128)}) custom-call(f32[256,256]{1,0:T(8,128)} %get-tuple-element.8.d_ref, f32[1,128]{1,0:T(1,128)} %get-tuple-element.9.c_ref, f32[256,256]{1,0:T(8,128)} %w_ref.1), custom_call_target="tpu_custom_call" | custom-call | tf_op jit(solution)/shard_map/pallas_call | solution.py:570

commit v3 on v2

--- a/solution.py
+++ b/solution.py
@@ -10,7 +10,7 @@
 F32 = jnp.float32
 BF16 = jnp.bfloat16
 MESH = pl.DeviceIdType.MESH
-WINDOW = 2
+WINDOW = 3
 
 
 def solve_system(system, zeta):
@@ -299,19 +299,17 @@
         send_row(r)
 
     forward(0)
-    forward(1)
     first()
 
     def body(r, _):
         forward(r)
-        later(r - 1)
+        later(r)
         return 0
 
-    lax.fori_loop(2, R - 1, body, 0)
+    lax.fori_loop(1, R - 1, body, 0)
     forward(R - 1, last=True)
     for j in range(1, X):
         p_send(j).start()
-    later(R - 2)
     later(R - 1)
 
     stored[p] = prev[chunk(z), :]
@@ -430,16 +428,10 @@
     damp = jnp.where(sub == col, 0.002, 0.0) + 1.0 / W
     zeta = esort[:, 0:1] - 0.9 * acc[:, W : W + 1]
     m = jnp.where(col == W, zeta, acc + damp)
-    for k in range(0, W, 2):
-        r0, r1 = m[k : k + 1, :], m[k + 1 : k + 2, :]
-        c0, c1 = m[:, k : k + 1], m[:, k + 1 : k + 2]
-        up, low = r0[:, k + 1 : k + 2], r1[:, k : k + 1]
-        inv0 = 1.0 / r0[:, k : k + 1]
-        ratio = up * inv0
-        inv1 = 1.0 / (r1[:, k + 1 : k + 2] - low * ratio)
-        p1 = (r1 - (low * inv0) * r0) * inv1
-        p0 = r0 * inv0 - ratio * p1
-        m = jnp.where(sub == k, p0, jnp.where(sub == k + 1, p1, m - c0 * p0 - c1 * p1))
+    for k in range(W):
+        pivot_row = m[k : k + 1, :]
+        pivot_row = pivot_row / pivot_row[:, k : k + 1]
+        m = jnp.where(sub == k, pivot_row, m - m[:, k : k + 1] * pivot_row)
     solved = jnp.broadcast_to(m[:, W : W + 1], (W, 128))
     csol[...] = solved
     sub = lax.broadcasted_iota(jnp.int32, (W, 128), 0)

time: 81.8 us -> 76.8 us (0.939)
  Pallas kernels: 81 us -> 76 us
    pallas_call x1, Pallas kernels: 79.2 us -> 74.1 us  [fused_shards(): pl.pallas_call(functools.partial(kernel, Z=Z, PP=PP), out_shape=(jax.Shap...]
where the time goes in v3:
time: 76.8 us; the launch traced here: 76.6 us
  Pallas kernels  76 us (99%)
    pallas_call x1, Pallas kernels, fused_shards(): pl.pallas_call(functools.partial(kernel, Z=Z, PP=PP), out_shape=(jax.Shap...  74.1 us
    pallas_call x1, Pallas kernels, fused_shards(): pl.pallas_call(finish, out_shape=(jax.ShapeDtypeStruct((D, O), F32), jax....  1.86 us

profile of v3, /device:TPU:0, one launch (start us, length us, event | category | flops | bytes accessed | tf_op | source)
XLA Modules:
  0.0 76.6 jit_solution(3715714917943735139)
XLA Ops:
  0.6 74.1 %shard_map.94 = (f32[256,256]{1,0:T(8,128)}, f32[1,128]{1,0:T(1,128)}) custom-call(bf16[12,256,256]{2,1,0:T(8,128)(2,1)} %act.1, bf16[12,256,1024]{2,1,0:T(8,128)(2,1)} %cot.1, f32[256,256]{1,0:T(8,128)} %prev_in.1, s32[1,1024]{1,0:T(1,128)} %bitcast.4, f32[1,12]{1,0:T(1,128)} %bitcast.5, s32[1,12]{1,0:T(1,128)} %bitcast.6), custom_call_target="tpu_custom_call" | custom-call | flops 1610612736 | bytes 12582912 | tf_op jit(solution)/shard_map/pallas_call | solution.py:499
  74.8 1.9 %shard_map.95 = (f32[256,256]{1,0:T(8,128)}, f32[256,256]{1,0:T(8,128)}, f32[1,12]{1,0:T(1,128)}) custom-call(f32[256,256]{1,0:T(8,128)} %get-tuple-element.8.d_ref, f32[1,128]{1,0:T(1,128)} %get-tuple-element.9.c_ref, f32[256,256]{1,0:T(8,128)} %w_ref.1), custom_call_target="tpu_custom_call" | custom-call | tf_op jit(solution)/shard_map/pallas_call | solution.py:562

commit v4 on v3

--- a/solution.py
+++ b/solution.py
@@ -380,8 +380,8 @@
     def gram_step(i, carry):
         gram, proj = carry
         parts = []
-        for u in range(4):
-            d = i * 4 + u
+        for u in range(16):
+            d = i * 16 + u
             row = jnp.concatenate(
                 [cent[h, pl.ds(d, W, stride=dc), :] for h in range(halves)], axis=1
             )
@@ -395,7 +395,7 @@
         return gram, proj
 
     gram, proj = lax.fori_loop(
-        0, dc // 4, gram_step, (jnp.zeros((W, W), F32), jnp.zeros((W, O), F32))
+        0, dc // 16, gram_step, (jnp.zeros((W, W), F32), jnp.zeros((W, O), F32))
     )
     whole = jnp.concatenate(
         [gram, jnp.sum(proj, axis=1, keepdims=True), jnp.zeros((W, L - W - 1), F32)], axis=1

time: 76.8 us -> 75.3 us (0.980)
  Pallas kernels: 76 us -> 74.5 us
    pallas_call x1, Pallas kernels: 74.1 us -> 72.6 us  [fused_shards(): pl.pallas_call(functools.partial(kernel, Z=Z, PP=PP), out_shape=(jax.Shap...]
where the time goes in v4:
time: 75.3 us; the launch traced here: 75.1 us
  Pallas kernels  74.5 us (99%)
    pallas_call x1, Pallas kernels, fused_shards(): pl.pallas_call(functools.partial(kernel, Z=Z, PP=PP), out_shape=(jax.Shap...  72.6 us
    pallas_call x1, Pallas kernels, fused_shards(): pl.pallas_call(finish, out_shape=(jax.ShapeDtypeStruct((D, O), F32), jax....  1.86 us

profile of v4, /device:TPU:0, one launch (start us, length us, event | category | flops | bytes accessed | tf_op | source)
XLA Modules:
  0.0 75.1 jit_solution(14524583676564744097)
XLA Ops:
  0.6 72.6 %shard_map.94 = (f32[256,256]{1,0:T(8,128)}, f32[1,128]{1,0:T(1,128)}) custom-call(bf16[12,256,256]{2,1,0:T(8,128)(2,1)} %act.1, bf16[12,256,1024]{2,1,0:T(8,128)(2,1)} %cot.1, f32[256,256]{1,0:T(8,128)} %prev_in.1, s32[1,1024]{1,0:T(1,128)} %bitcast.4, f32[1,12]{1,0:T(1,128)} %bitcast.5, s32[1,12]{1,0:T(1,128)} %bitcast.6), custom_call_target="tpu_custom_call" | custom-call | flops 1610612736 | bytes 12582912 | tf_op jit(solution)/shard_map/pallas_call | solution.py:499
  73.2 1.9 %shard_map.95 = (f32[256,256]{1,0:T(8,128)}, f32[256,256]{1,0:T(8,128)}, f32[1,12]{1,0:T(1,128)}) custom-call(f32[256,256]{1,0:T(8,128)} %get-tuple-element.8.d_ref, f32[1,128]{1,0:T(1,128)} %get-tuple-element.9.c_ref, f32[256,256]{1,0:T(8,128)} %w_ref.1), custom_call_target="tpu_custom_call" | custom-call | tf_op jit(solution)/shard_map/pallas_call | solution.py:562
